TPU v7x, 32 devices: a whole 2x2x4 slice. The times are simulated.
32 devices in a mesh: patch: 8 (over z, x), lag: 4 (over y, core).
Axes of the slice: x: 2, y: 2, z: 4, core: 2. Of those that a mesh axis runs over, the one named last changes fastest.
Arguments:
- history: bfloat16 [4, 128, 8192], P('lag', None, 'patch'), may hold values from -6 to 6
- coupling: bfloat16 [4, 8192, 1024], P('lag', 'patch'), may hold values from -0.09375 to 0.09375
- inverse: bfloat16 [8192, 1024], P('patch'), may hold values from -0.1875 to 0.1875
- cotangent: bfloat16 [6, 128, 8192], P(None, 'lag', 'patch'), may hold values from -6 to 6
- targets: int32 [4, 8], P('lag'), may hold values from 0 to 7
Outputs:
- adjoint: bfloat16 [6, 128, 8192], P(None, 'lag', 'patch')
Inputs may be any that keep to these rules, and one draw needn't show every extreme that they name: `targets`: each lag and source patch lists exactly one target patch; several sources may list the same target.
All inputs are finite; a program needn't handle non-finite values.
Results may differ from a plain program's by a relative error of at most 0.0085.
Values may be sent and summed in bfloat16 or wider, within the bound.
A program may use at most 64 MiB of HBM per device.

v0:
```python
import jax
import jax.numpy as jnp
from jax import lax
from jax.sharding import PartitionSpec as P

STEPS = 6


def passed_along(value, axis, by):
    size = lax.axis_size(axis)
    pairs = [(i, i + by) for i in range(size) if 0 <= i + by < size]
    return lax.ppermute(value, axis, pairs)


def on_device(history, coupling, inverse, cotangent, targets):
    history_now = history[0]
    coupling_tile = coupling[0]
    target_row = targets[0]
    patch_count = lax.axis_size("patch")
    rows_total = history_now.shape[0]
    unknowns = history_now.shape[1]
    block_rows = rows_total // patch_count
    lag_index = lax.axis_index("lag")
    results = []
    for turn_index in range(STEPS):
        pieces = lax.all_to_all(
            history_now.reshape(patch_count, block_rows, unknowns),
            "patch",
            split_axis=0,
            concat_axis=0,
            tiled=True,
        )
        chosen = jnp.take(pieces, target_row, axis=0)
        partial_value = jnp.einsum(
            "prj,jk->prk",
            lax.all_to_all(chosen, "patch", split_axis=0, concat_axis=0, tiled=True),
            coupling_tile,
            preferred_element_type=jnp.float32,
        )
        partial_value = partial_value.reshape(rows_total, unknowns)
        summed = lax.psum_scatter(partial_value, "lag", scatter_dimension=0, tiled=True)
        residual = (cotangent[turn_index].astype(jnp.float32) - summed).astype(jnp.bfloat16)
        own_rows = jnp.dot(residual, inverse, preferred_element_type=jnp.float32).astype(
            jnp.bfloat16
        )
        if turn_index + 1 < STEPS:
            latest = lax.all_gather(own_rows, "lag", axis=0, tiled=True)
        results.append(own_rows)
        if turn_index + 1 < STEPS:
            shifted = passed_along(history_now, "lag", 1)
            history_now = jnp.where(lag_index == 0, latest, shifted)
    return jnp.stack(results)


def solution(mesh):
    placed = (
        P("lag", None, "patch"),
        P("lag", "patch", None),
        P("patch", None),
        P(None, "lag", "patch"),
        P("lag", None),
    )
    return jax.shard_map(
        on_device, mesh=mesh, in_specs=placed, out_specs=P(None, "lag", "patch"), check_vma=False
    )
```

profile of v0, /device:TPU:0, one launch (start us, length us, event | category | flops | bytes accessed | tf_op | source)
XLA Modules:
  0.0 359.9 jit_solution(12010703531544779589)
XLA Ops:
  6.5 7.4 %all-to-all-start = ((bf16[8,16,1024]{2,1,0:T(8,128)(2,1)}), bf16[8,16,1024]{2,1,0:T(8,128)(2,1)S(1)}, u32[]{:S(2)}, u32[]{:S(2)}) async-start(bf16[8,16,1024]{2,1,0:T(8,128)(2,1)} %bitcast.113), calls=%async_computation | async-start | bytes 524288 | tf_op jit(solution)/shard_map/all_to_all | solution.py:26
  14.0 0.7 compare_select_fusion
  14.6 0.7 compare_and_fusion
  15.3 7.5 %all-to-all-done = bf16[8,16,1024]{2,1,0:T(8,128)(2,1)S(1)} async-done(((bf16[8,16,1024]{2,1,0:T(8,128)(2,1)}), bf16[8,16,1024]{2,1,0:T(8,128)(2,1)S(1)}, u32[]{:S(2)}, u32[]{:S(2)}) %all-to-all-start) | async-done | bytes 262176 | tf_op jit(solution)/shard_map/all_to_all | solution.py:26
  22.8 0.6 gather_fusion
  23.5 12.1 %all_to_all.60 = bf16[8,16,1024]{2,1,0:T(8,128)(2,1)S(1)} all-to-all(bf16[8,16,1024]{2,1,0:T(8,128)(2,1)S(1)} %broadcast_select_fusion.5), channel_id=1, replica_groups=mesh['patch'=8,'lag'=4] {'patch'}, dimensions={0} | all-to-all | bytes 524288 | tf_op jit(solution)/shard_map/all_to_all | solution.py:36
  35.6 2.8 fusion.10
  38.5 1.3 collective-permute-start
  39.9 19.5 %reduce-scatter.7.cloned.1.call-done = f32[32,1024]{1,0:T(8,128)} async-done(((f32[128,1024]{1,0:T(8,128)}), f32[32,1024]{1,0:T(8,128)}) %reduce-scatter.7.cloned.1.call-update) | async-done | bytes 131088 | tf_op jit(solution)/shard_map/reduce_scatter | solution.py:41
  59.3 2.0 bitcast_dynamic-update-slice_fusion.4
  61.3 5.8 %all_gather.15 = bf16[128,1024]{1,0:T(8,128)(2,1)S(1)} all-gather(bf16[32,1024]{1,0:T(8,128)(2,1)S(1)} %get-tuple-element.7), channel_id=1, replica_groups=mesh['patch'=8,'lag'=4] {'lag'}, dimensions={0}, use_global_device_ids=true | all-gather | bytes 327680 | tf_op jit(solution)/shard_map/all_gather | solution.py:47
  67.1 14.7 %all_to_all.61 = bf16[8,16,1024]{2,1,0:T(8,128)(2,1)S(1)} all-to-all(bf16[8,16,1024]{2,1,0:T(8,128)(2,1)S(1)} %bitcast.102), channel_id=1, replica_groups=mesh['patch'=8,'lag'=4] {'patch'}, dimensions={0} | all-to-all | bytes 524288 | tf_op jit(solution)/shard_map/all_to_all | solution.py:26
  81.9 0.6 gather_fusion.1
  82.5 12.4 %all_to_all.62 = bf16[8,16,1024]{2,1,0:T(8,128)(2,1)S(1)} all-to-all(bf16[8,16,1024]{2,1,0:T(8,128)(2,1)S(1)} %broadcast_select_fusion.4), channel_id=1, replica_groups=mesh['patch'=8,'lag'=4] {'patch'}, dimensions={0} | all-to-all | bytes 524288 | tf_op jit(solution)/shard_map/all_to_all | solution.py:36
  94.9 2.8 fusion.8
  97.8 1.3 collective-permute-start.1
  99.1 18.5 %reduce-scatter.9.cloned.1.call-done = f32[32,1024]{1,0:T(8,128)} async-done(((f32[128,1024]{1,0:T(8,128)}), f32[32,1024]{1,0:T(8,128)}) %reduce-scatter.9.cloned.1.call-update) | async-done | bytes 131088 | tf_op jit(solution)/shard_map/reduce_scatter | solution.py:41
  117.7 2.0 bitcast_dynamic-update-slice_fusion.3
  119.7 5.8 %all_gather.16 = bf16[128,1024]{1,0:T(8,128)(2,1)S(1)} all-gather(bf16[32,1024]{1,0:T(8,128)(2,1)S(1)} %get-tuple-element.9), channel_id=1, replica_groups=mesh['patch'=8,'lag'=4] {'lag'}, dimensions={0}, use_global_device_ids=true | all-gather | bytes 327680 | tf_op jit(solution)/shard_map/all_gather | solution.py:47
  125.5 14.7 %all_to_all.63 = bf16[8,16,1024]{2,1,0:T(8,128)(2,1)S(1)} all-to-all(bf16[8,16,1024]{2,1,0:T(8,128)(2,1)S(1)} %bitcast.103), channel_id=1, replica_groups=mesh['patch'=8,'lag'=4] {'patch'}, dimensions={0} | all-to-all | bytes 524288 | tf_op jit(solution)/shard_map/all_to_all | solution.py:26
  140.2 0.6 gather_fusion.2
  140.9 12.4 %all_to_all.64 = bf16[8,16,1024]{2,1,0:T(8,128)(2,1)S(1)} all-to-all(bf16[8,16,1024]{2,1,0:T(8,128)(2,1)S(1)} %broadcast_select_fusion.3), channel_id=1, replica_groups=mesh['patch'=8,'lag'=4] {'patch'}, dimensions={0} | all-to-all | bytes 524288 | tf_op jit(solution)/shard_map/all_to_all | solution.py:36
  153.3 2.8 fusion.6
  156.2 1.3 collective-permute-start.2
  157.5 18.5 %reduce-scatter.11.cloned.1.call-done = f32[32,1024]{1,0:T(8,128)} async-done(((f32[128,1024]{1,0:T(8,128)}), f32[32,1024]{1,0:T(8,128)}) %reduce-scatter.11.cloned.1.call-update) | async-done | bytes 131088 | tf_op jit(solution)/shard_map/reduce_scatter | solution.py:41
  176.0 2.0 bitcast_dynamic-update-slice_fusion.2
  178.0 5.8 %all_gather.17 = bf16[128,1024]{1,0:T(8,128)(2,1)S(1)} all-gather(bf16[32,1024]{1,0:T(8,128)(2,1)S(1)} %get-tuple-element.11), channel_id=1, replica_groups=mesh['patch'=8,'lag'=4] {'lag'}, dimensions={0}, use_global_device_ids=true | all-gather | bytes 327680 | tf_op jit(solution)/shard_map/all_gather | solution.py:47
  183.9 14.7 %all_to_all.65 = bf16[8,16,1024]{2,1,0:T(8,128)(2,1)S(1)} all-to-all(bf16[8,16,1024]{2,1,0:T(8,128)(2,1)S(1)} %bitcast.104), channel_id=1, replica_groups=mesh['patch'=8,'lag'=4] {'patch'}, dimensions={0} | all-to-all | bytes 524288 | tf_op jit(solution)/shard_map/all_to_all | solution.py:26
  198.6 0.6 gather_fusion.3
  199.2 12.4 %all_to_all.66 = bf16[8,16,1024]{2,1,0:T(8,128)(2,1)S(1)} all-to-all(bf16[8,16,1024]{2,1,0:T(8,128)(2,1)S(1)} %broadcast_select_fusion.2), channel_id=1, replica_groups=mesh['patch'=8,'lag'=4] {'patch'}, dimensions={0} | all-to-all | bytes 524288 | tf_op jit(solution)/shard_map/all_to_all | solution.py:36
  211.6 2.8 fusion.4
  214.5 1.3 collective-permute-start.3
  215.9 18.5 %reduce-scatter.13.cloned.1.call-done = f32[32,1024]{1,0:T(8,128)} async-done(((f32[128,1024]{1,0:T(8,128)}), f32[32,1024]{1,0:T(8,128)}) %reduce-scatter.13.cloned.1.call-update) | async-done | bytes 131088 | tf_op jit(solution)/shard_map/reduce_scatter | solution.py:41
  234.4 2.0 bitcast_dynamic-update-slice_fusion.1
  236.4 5.8 %all_gather.18 = bf16[128,1024]{1,0:T(8,128)(2,1)S(1)} all-gather(bf16[32,1024]{1,0:T(8,128)(2,1)S(1)} %get-tuple-element.13), channel_id=1, replica_groups=mesh['patch'=8,'lag'=4] {'lag'}, dimensions={0}, use_global_device_ids=true | all-gather | bytes 327680 | tf_op jit(solution)/shard_map/all_gather | solution.py:47
  242.2 14.7 %all_to_all.67 = bf16[8,16,1024]{2,1,0:T(8,128)(2,1)S(1)} all-to-all(bf16[8,16,1024]{2,1,0:T(8,128)(2,1)S(1)} %bitcast.105), channel_id=1, replica_groups=mesh['patch'=8,'lag'=4] {'patch'}, dimensions={0} | all-to-all | bytes 524288 | tf_op jit(solution)/shard_map/all_to_all | solution.py:26
  256.9 0.6 gather_fusion.4
  257.6 12.4 %all_to_all.68 = bf16[8,16,1024]{2,1,0:T(8,128)(2,1)S(1)} all-to-all(bf16[8,16,1024]{2,1,0:T(8,128)(2,1)S(1)} %broadcast_select_fusion.1), channel_id=1, replica_groups=mesh['patch'=8,'lag'=4] {'patch'}, dimensions={0} | all-to-all | bytes 524288 | tf_op jit(solution)/shard_map/all_to_all | solution.py:36
  270.0 2.8 fusion.2
  272.9 1.3 collective-permute-start.4
  274.2 18.5 %reduce-scatter.15.cloned.1.call-done = f32[32,1024]{1,0:T(8,128)} async-done(((f32[128,1024]{1,0:T(8,128)}), f32[32,1024]{1,0:T(8,128)}) %reduce-scatter.15.cloned.1.call-update) | async-done | bytes 131088 | tf_op jit(solution)/shard_map/reduce_scatter | solution.py:41
  292.8 2.0 bitcast_dynamic-update-slice_fusion
  294.8 5.8 %all_gather.19 = bf16[128,1024]{1,0:T(8,128)(2,1)S(1)} all-gather(bf16[32,1024]{1,0:T(8,128)(2,1)S(1)} %get-tuple-element.15), channel_id=1, replica_groups=mesh['patch'=8,'lag'=4] {'lag'}, dimensions={0}, use_global_device_ids=true | all-gather | bytes 327680 | tf_op jit(solution)/shard_map/all_gather | solution.py:47
  300.6 14.7 %all_to_all.69 = bf16[8,16,1024]{2,1,0:T(8,128)(2,1)S(1)} all-to-all(bf16[8,16,1024]{2,1,0:T(8,128)(2,1)S(1)} %bitcast.106), channel_id=1, replica_groups=mesh['patch'=8,'lag'=4] {'patch'}, dimensions={0} | all-to-all | bytes 524288 | tf_op jit(solution)/shard_map/all_to_all | solution.py:26
  316.0 12.4 %all_to_all.70 = bf16[8,16,1024]{2,1,0:T(8,128)(2,1)S(1)} all-to-all(bf16[8,16,1024]{2,1,0:T(8,128)(2,1)S(1)} %broadcast_select_fusion), channel_id=1, replica_groups=mesh['patch'=8,'lag'=4] {'patch'}, dimensions={0} | all-to-all | bytes 524288 | tf_op jit(solution)/shard_map/all_to_all | solution.py:36
  328.3 2.8 fusion
  331.2 19.9 %reduce-scatter.17.cloned.1.call-done = f32[32,1024]{1,0:T(8,128)} async-done(((f32[128,1024]{1,0:T(8,128)}), f32[32,1024]{1,0:T(8,128)}) %reduce-scatter.17.cloned.1.call-update) | async-done | bytes 131088 | tf_op jit(solution)/shard_map/reduce_scatter | solution.py:41
  351.1 2.0 fusion.13
  (36 shorter events, 1.6 us)
Async XLA Ops:
  6.5 52.8 %copy-start = (bf16[1024,1024]{1,0:T(8,128)(2,1)S(1)}, bf16[1024,1024]{1,0:T(8,128)(2,1)}, u32[]{:S(2)}) copy-start(bf16[1024,1024]{1,0:T(8,128)(2,1)} %param.9) | copy-start | bytes 6291460
  6.5 16.3 %all-to-all-start = ((bf16[8,16,1024]{2,1,0:T(8,128)(2,1)}), bf16[8,16,1024]{2,1,0:T(8,128)(2,1)S(1)}, u32[]{:S(2)}, u32[]{:S(2)}) async-start(bf16[8,16,1024]{2,1,0:T(8,128)(2,1)} %bitcast.113), calls=%async_computation | async-start | bytes 524288 | tf_op jit(solution)/shard_map/all_to_all | solution.py:26
  13.9 45.4 %reduce-scatter.7.cloned.1.call-start = ((), (), s32[]{:S(2)}) async-start(), calls=%async_computation.18 | async-start | bytes 655360 | tf_op jit(solution)/shard_map/reduce_scatter | solution.py:41
  23.5 15.0 %copy-start.2 = (bf16[1,128,1024]{2,1,0:T(8,128)(2,1)S(1)}, bf16[1,128,1024]{2,1,0:T(8,128)(2,1)}, u32[]{:S(2)}) copy-start(bf16[1,128,1024]{2,1,0:T(8,128)(2,1)} %param.7) | copy-start | bytes 786436
  23.5 35.8 %copy-start.1 = (bf16[6,32,1024]{2,1,0:T(8,128)(2,1)S(1)}, bf16[6,32,1024]{2,1,0:T(8,128)(2,1)}, u32[]{:S(2)}) copy-start(bf16[6,32,1024]{2,1,0:T(8,128)(2,1)} %param.10) | copy-start | bytes 1179652
  38.5 79.2 %reduce-scatter.9.cloned.1.call-start = ((), (), s32[]{:S(2)}) async-start(), calls=%async_computation.19 | async-start | bytes 655360 | tf_op jit(solution)/shard_map/reduce_scatter | solution.py:41
  38.5 28.6 %collective-permute-start = (bf16[128,1024]{1,0:T(8,128)(2,1)S(1)}, bf16[128,1024]{1,0:T(8,128)(2,1)S(1)}, u32[]{:S(2)}, u32[]{:S(2)}) collective-permute-start(bf16[128,1024]{1,0:T(8,128)(2,1)S(1)} %bitcast.114), channel_id=1, source_target_pairs={{0,1},{1,2},{2,3},{4,5},{5,6},{6,7},{8,9},{9,10},{10,11},{12,13},{... | collective-permute-start | bytes 786440 | tf_op jit(solution)/shard_map/ppermute | solution.py:12
  97.8 78.3 %reduce-scatter.11.cloned.1.call-start = ((), (), s32[]{:S(2)}) async-start(), calls=%async_computation.20 | async-start | bytes 655360 | tf_op jit(solution)/shard_map/reduce_scatter | solution.py:41
  97.8 27.6 %collective-permute-start.1 = (bf16[128,1024]{1,0:T(8,128)(2,1)S(1)}, bf16[128,1024]{1,0:T(8,128)(2,1)S(1)}, u32[]{:S(2)}, u32[]{:S(2)}) collective-permute-start(bf16[128,1024]{1,0:T(8,128)(2,1)S(1)} %broadcast_select_fusion.10), channel_id=1, source_target_pairs={{0,1},{1,2},{2,3},{4,5},{5,6},{6,7},{8,9},{9,10},{10,11},{12,13},{... | collective-permute-start | bytes 786440 | tf_op jit(solution)/shard_map/ppermute | solution.py:12
  156.2 78.2 %reduce-scatter.13.cloned.1.call-start = ((), (), s32[]{:S(2)}) async-start(), calls=%async_computation.21 | async-start | bytes 655360 | tf_op jit(solution)/shard_map/reduce_scatter | solution.py:41
  156.2 27.6 %collective-permute-start.2 = (bf16[128,1024]{1,0:T(8,128)(2,1)S(1)}, bf16[128,1024]{1,0:T(8,128)(2,1)S(1)}, u32[]{:S(2)}, u32[]{:S(2)}) collective-permute-start(bf16[128,1024]{1,0:T(8,128)(2,1)S(1)} %broadcast_select_fusion.9), channel_id=1, source_target_pairs={{0,1},{1,2},{2,3},{4,5},{5,6},{6,7},{8,9},{9,10},{10,11},{12,13},{... | collective-permute-start | bytes 786440 | tf_op jit(solution)/shard_map/ppermute | solution.py:12
  214.5 78.3 %reduce-scatter.15.cloned.1.call-start = ((), (), s32[]{:S(2)}) async-start(), calls=%async_computation.22 | async-start | bytes 655360 | tf_op jit(solution)/shard_map/reduce_scatter | solution.py:41
  214.5 27.6 %collective-permute-start.3 = (bf16[128,1024]{1,0:T(8,128)(2,1)S(1)}, bf16[128,1024]{1,0:T(8,128)(2,1)S(1)}, u32[]{:S(2)}, u32[]{:S(2)}) collective-permute-start(bf16[128,1024]{1,0:T(8,128)(2,1)S(1)} %broadcast_select_fusion.8), channel_id=1, source_target_pairs={{0,1},{1,2},{2,3},{4,5},{5,6},{6,7},{8,9},{9,10},{10,11},{12,13},{... | collective-permute-start | bytes 786440 | tf_op jit(solution)/shard_map/ppermute | solution.py:12
  272.9 78.2 %reduce-scatter.17.cloned.1.call-start = ((), (), s32[]{:S(2)}) async-start(), calls=%async_computation.23 | async-start | bytes 655360 | tf_op jit(solution)/shard_map/reduce_scatter | solution.py:41
  272.9 27.6 %collective-permute-start.4 = (bf16[128,1024]{1,0:T(8,128)(2,1)S(1)}, bf16[128,1024]{1,0:T(8,128)(2,1)S(1)}, u32[]{:S(2)}, u32[]{:S(2)}) collective-permute-start(bf16[128,1024]{1,0:T(8,128)(2,1)S(1)} %broadcast_select_fusion.7), channel_id=1, source_target_pairs={{0,1},{1,2},{2,3},{4,5},{5,6},{6,7},{8,9},{9,10},{10,11},{12,13},{... | collective-permute-start | bytes 786440 | tf_op jit(solution)/shard_map/ppermute | solution.py:12
Sparse Core Ops, SparseCore 0:
  38.6 20.6 reduce-scatter.6
  97.9 19.7 reduce-scatter.8
  156.3 19.7 reduce-scatter.10
  214.6 19.7 reduce-scatter.12
  273.0 19.7 reduce-scatter.14
  331.3 19.7 reduce-scatter.16
where the time goes:
time: 361 us; the launch traced here: 360 us
  blocking collectives  176 us (49%)
  waiting for transfers between devices  121 us (34%)
  matrix products  29.1 us (8%)
  starting transfers between devices  14.2 us (4%)
  between operations  13.7 us (4%)
    reduce_scatter x6, waiting for transfers between devices, on_device(): lax.psum_scatter(partial_value, 'lag', scatter_dimension=0, tiled=True)  114 us
    all_to_all x6, blocking collectives, on_device(): lax.all_to_all(chosen, 'patch', split_axis=0, concat_axis=0, tiled=True)  74 us
    all_to_all x5, blocking collectives, on_device(): lax.all_to_all(history_now.reshape(patch_count, block_rows, unknowns), 'p...  73.6 us
    all_gather x5, blocking collectives, on_device(): latest = lax.all_gather(own_rows, 'lag', axis=0, tiled=True)  28.9 us
    dot_general x6, matrix products, on_device(): jnp.einsum('prj,jk->prk', lax.all_to_all(chosen, 'patch', split_axis=0, c...  17.1 us
    dot_general x6, matrix products, on_device(): jnp.dot(residual, inverse, preferred_element_type=jnp.float32)  12 us
    all_to_all x1, waiting for transfers between devices, on_device(): lax.all_to_all(history_now.reshape(patch_count, block_rows, unknowns), 'p...  7.54 us
    all_to_all x1, starting transfers between devices, on_device(): lax.all_to_all(history_now.reshape(patch_count, block_rows, unknowns), 'p...  7.38 us
  transfers between devices with their start and end apart: 12, of which 7 were waited for; matrix products, arithmetic and copies ran while one was open for 3% of the time, Pallas kernels for 0%

commit v1 on v0

v1 whole, which is shorter than its diff:
```python
import functools

import jax
import jax.numpy as jnp
from jax import lax
from jax.experimental import pallas as pl
from jax.experimental.pallas import tpu as pltpu
from jax.sharding import PartitionSpec as P

MESH = pl.DeviceIdType.MESH
LANES = 128


def kernel(
    patches, lags, steps, holders, width,
    history, coupling, inverse, cotangent, targets, out,
    held_start, staged_start, chosen, product, terms, states, held, current, staged, listed, listed_scalar,
    list_send, list_recv, list_local, start_send, start_recv, place_start_send, chosen_recv,
    term_send, term_recv, state_send, held_recv, place_send,
):
    patch = lax.axis_index("patch")
    lag = lax.axis_index("lag")
    rows = history.shape[1]
    unknowns = history.shape[2]
    depth = min(steps, lags)
    tile = min(unknowns, 256)

    def columns(index):
        return pl.ds(pl.multiple_of(index * width, LANES), width)

    def await_bytes(ref, semaphore):
        pltpu.make_async_copy(ref, ref, semaphore).wait()

    def send(src, dst, send_sem, recv_sem, to_patch, to_lag):
        pltpu.make_async_remote_copy(
            src_ref=src, dst_ref=dst, send_sem=send_sem, recv_sem=recv_sem,
            device_id=(to_patch, to_lag), device_id_type=MESH,
        ).start()

    barrier = pltpu.get_barrier_semaphore()
    own = patch * lags + lag

    @pl.loop(1, patches * lags)
    def _(offset):
        other = lax.rem(own + offset, patches * lags)
        pl.semaphore_signal(barrier, inc=1, device_id=(other // lags, lax.rem(other, lags)), device_id_type=MESH)

    pl.semaphore_wait(barrier, patches * lags - 1)

    @pl.loop(1, lags)
    def _(offset):
        to_lag = lax.rem(lag + offset, lags)
        send(targets, listed.at[lag], list_send, list_recv, patch, to_lag)

    @pl.loop(0, holders)
    def _(holder):
        @pl.when(holder != patch)
        def _():
            send(history.at[:, :, columns(holder)], held_start.at[patch], start_send, start_recv, holder, lag)

    listed[lag] = targets[...]

    @pl.when(patch < holders)
    def _():
        held_start[patch] = history[:, :, columns(patch)]

    await_bytes(listed.at[pl.ds(0, lags - 1)], list_recv)
    move = pltpu.make_async_copy(listed, listed_scalar, list_local)
    move.start()
    move.wait()

    @pl.when(patch < holders)
    def _():
        await_bytes(held_start.at[pl.ds(0, patches - 1)], start_recv)

        @pl.loop(0, depth)
        def _(step):
            to_lag = lag + step

            @pl.when(to_lag < lags)
            def _():
                @pl.loop(0, patches)
                def _(offset):
                    to_patch = lax.rem(patch + offset, patches)
                    staged_start[step, to_patch] = held_start[listed_scalar[to_lag, 0, to_patch]]
                    src = staged_start.at[step, to_patch]
                    dst = chosen.at[step, :, :, columns(patch)]
                    here = jnp.logical_and(step == 0, offset == 0)

                    @pl.when(here)
                    def _():
                        pltpu.make_async_copy(src, dst, chosen_recv.at[step]).start()

                    @pl.when(jnp.logical_not(here))
                    def _():
                        send(src, dst, place_start_send.at[step], chosen_recv.at[step], to_patch, to_lag)

    @pl.loop(0, steps)
    def _(step):
        await_bytes(chosen.at[step], chosen_recv.at[step])
        picked = chosen[step].reshape(lags * rows, unknowns)
        for first in range(0, unknowns, tile):
            part = jnp.dot(picked, coupling[0, :, first:first + tile], preferred_element_type=jnp.float32)
            product[step, :, :, first:first + tile] = part.astype(jnp.bfloat16).reshape(lags, rows, tile)

        @pl.loop(1, lags)
        def _(offset):
            to_lag = lax.rem(lag + offset, lags)
            send(product.at[step, to_lag], terms.at[step, lag], term_send.at[step], term_recv.at[step], patch, to_lag)

        total = cotangent[step].astype(jnp.float32) - product[step, lag].astype(jnp.float32)
        await_bytes(terms.at[step, pl.ds(0, lags - 1)], term_recv.at[step])
        for offset in range(1, lags):
            total = total - terms[step, lax.rem(lag + offset, lags)].astype(jnp.float32)
        residual = total.astype(jnp.bfloat16)
        for first in range(0, unknowns, tile):
            state = jnp.dot(residual, inverse[:, first:first + tile], preferred_element_type=jnp.float32)
            states[step, :, first:first + tile] = state.astype(jnp.bfloat16)
        out[step] = states[step]

        @pl.when(step + 1 < steps)
        def _():
            @pl.loop(0, holders)
            def _(holder):
                @pl.when(holder != patch)
                def _():
                    send(
                        states.at[step, :, columns(holder)], held.at[step, patch],
                        state_send.at[step], held_recv.at[step], holder, lag,
                    )

            @pl.when(patch < holders)
            def _():
                held[step, patch] = states[step, :, columns(patch)]
                await_bytes(held.at[step, pl.ds(0, patches - 1)], held_recv.at[step])
                current[...] = held[step]

                @pl.loop(0, lags)
                def _(to_lag):
                    later = step + 1 + to_lag

                    @pl.when(later < steps)
                    def _():
                        @pl.loop(0, patches)
                        def _(offset):
                            to_patch = lax.rem(patch + offset, patches)
                            staged[step, to_lag, to_patch] = current[listed_scalar[to_lag, 0, to_patch]]
                            src = staged.at[step, to_lag, to_patch]
                            dst = chosen.at[later, lag, :, columns(patch)]
                            here = jnp.logical_and(to_lag == lag, offset == 0)

                            @pl.when(here)
                            def _():
                                pltpu.make_async_copy(src, dst, chosen_recv.at[later]).start()

                            @pl.when(jnp.logical_not(here))
                            def _():
                                send(src, dst, place_send.at[step, to_lag], chosen_recv.at[later], to_patch, to_lag)

    await_bytes(listed.at[pl.ds(0, lags - 1)], list_send)

    def drained(ref, count_here, count_else, semaphore):
        @pl.when(patch < holders)
        def _():
            await_bytes(ref.at[pl.ds(0, count_here)], semaphore)

        if holders < patches:
            @pl.when(patch >= holders)
            def _():
                await_bytes(ref.at[pl.ds(0, count_else)], semaphore)

    drained(held_start, holders - 1, holders, start_send)

    @pl.when(patch < holders)
    def _():
        @pl.loop(0, depth)
        def _(step):
            @pl.when(lag + step < lags)
            def _():
                @pl.when(step == 0)
                def _():
                    await_bytes(staged_start.at[step, pl.ds(0, patches - 1)], place_start_send.at[step])

                @pl.when(step > 0)
                def _():
                    await_bytes(staged_start.at[step], place_start_send.at[step])

    @pl.loop(0, steps)
    def _(step):
        await_bytes(product.at[step, pl.ds(0, lags - 1)], term_send.at[step])

        @pl.when(step + 1 < steps)
        def _():
            drained(held.at[step], holders - 1, holders, state_send.at[step])

            @pl.when(patch < holders)
            def _():
                @pl.loop(0, lags)
                def _(to_lag):
                    @pl.when(step + 1 + to_lag < steps)
                    def _():
                        @pl.when(to_lag == lag)
                        def _():
                            await_bytes(staged.at[step, to_lag, pl.ds(0, patches - 1)], place_send.at[step, to_lag])

                        @pl.when(to_lag != lag)
                        def _():
                            await_bytes(staged.at[step, to_lag], place_send.at[step, to_lag])


def on_device(patches, lags, history, coupling, inverse, cotangent, targets):
    steps, rows, unknowns = cotangent.shape
    holders = min(patches, max(1, unknowns // LANES))
    width = unknowns // holders
    depth = min(steps, lags)
    vmem = pl.BlockSpec(memory_space=pltpu.VMEM)
    kind = history.dtype
    dma = pltpu.SemaphoreType.DMA
    return pl.pallas_call(
        functools.partial(kernel, patches, lags, steps, holders, width),
        out_shape=jax.ShapeDtypeStruct((steps, rows, unknowns), kind),
        in_specs=[vmem] * 5,
        out_specs=vmem,
        scratch_shapes=[
            pltpu.VMEM((patches, lags, rows, width), kind),
            pltpu.VMEM((depth, patches, lags, rows, width), kind),
            pltpu.VMEM((steps, lags, rows, unknowns), kind),
            pltpu.VMEM((steps, lags, rows, unknowns), kind),
            pltpu.VMEM((steps, lags, rows, unknowns), kind),
            pltpu.VMEM((steps, rows, unknowns), kind),
            pltpu.VMEM((steps, patches, rows, width), kind),
            pltpu.VMEM((patches, rows, width), kind),
            pltpu.VMEM((steps, lags, patches, rows, width), kind),
            pltpu.VMEM((lags, 1, patches), jnp.int32),
            pltpu.SMEM((lags, 1, patches), jnp.int32),
            dma, dma, dma, dma, dma, dma((depth,)), dma((steps,)),
            dma((steps,)), dma((steps,)), dma((steps,)), dma((steps,)), dma((steps, lags)),
        ],
        compiler_params=pltpu.CompilerParams(
            collective_id=0, has_side_effects=True, vmem_limit_bytes=48 * 1024 * 1024
        ),
    )(history.reshape(lags, rows, unknowns), coupling, inverse, cotangent, targets)


def solution(mesh):
    placed = (
        P("lag", None, "patch"),
        P("lag", "patch", None),
        P("patch", None),
        P(None, "lag", "patch"),
        P("lag", None),
    )
    return jax.shard_map(
        functools.partial(on_device, mesh.shape["patch"], mesh.shape["lag"]),
        mesh=mesh, in_specs=placed, out_specs=P(None, "lag", "patch"), check_vma=False,
    )
```

time: 361 us -> 111 us (0.31)
  blocking collectives: 176 us -> 0 us
  waiting for transfers between devices: 121 us -> 0 us
  Pallas kernels: 0 us -> 104 us
  matrix products: 29.1 us -> 0 us
  starting transfers between devices: 14.2 us -> 0 us
  between operations: 13.7 us -> 0.01 us
    all_to_all x11 -> x0, blocking collectives: 148 us -> none  [the longest x6 74 us: on_device(): lax.all_to_all(chosen, 'patch', split_axis=0, concat_axis=0, tiled=True)]
    reduce_scatter x6 -> x0, waiting for transfers between devices: 114 us -> none  [on_device(): lax.psum_scatter(partial_value, 'lag', scatter_dimension=0, tiled=True)]
    pallas_call x0 -> x1, Pallas kernels: none -> 104 us  [on_device(): pl.pallas_call(functools.partial(kernel, patches, lags, steps, holders, w...]
    dot_general x12 -> x0, matrix products: 29.1 us -> none  [the longest x6 17.1 us: on_device(): jnp.einsum('prj,jk->prk', lax.all_to_all(chosen, 'patch', split_axis=0, c...]
    all_gather x5 -> x0, blocking collectives: 28.9 us -> none  [on_device(): latest = lax.all_gather(own_rows, 'lag', axis=0, tiled=True)]
    all_to_all x1 -> x0, waiting for transfers between devices: 7.54 us -> none  [on_device(): lax.all_to_all(history_now.reshape(patch_count, block_rows, unknowns), 'p...]
    all_to_all x1 -> x0, starting transfers between devices: 7.38 us -> none  [on_device(): lax.all_to_all(history_now.reshape(patch_count, block_rows, unknowns), 'p...]
    ppermute x5 -> x0, starting transfers between devices: 6.53 us -> none  [passed_along(): return lax.ppermute(value, axis, pairs)]
  transfers between devices with their start and end apart: 12 -> 0, of which waited for: 7 -> 0; matrix products, arithmetic and copies ran while one was open for 3% -> 0% of each run, Pallas kernels for 0% -> 0%
where the time goes in v1:
time: 111 us; the launch traced here: 110 us
  Pallas kernels  104 us (94%)
  local copies, waits for them, and re-layouts  6.53 us (6%)
    pallas_call x1, Pallas kernels, on_device(): pl.pallas_call(functools.partial(kernel, patches, lags, steps, holders, w...  104 us
    unnamed x11, local copies, waits for them, and re-layouts  6.53 us

profile of v1, /device:TPU:0, one launch (start us, length us, event | category | flops | bytes accessed | tf_op | source)
XLA Modules:
  0.0 110.5 jit_solution(12820970082974415877)
XLA Ops:
  0.0 0.0 copy-start
  0.0 1.6 %copy-done = bf16[1,1024,1024]{2,1,0:T(8,128)(2,1)S(1)} copy-done((bf16[1,1024,1024]{2,1,0:T(8,128)(2,1)S(1)}, bf16[1,1024,1024]{2,1,0:T(8,128)(2,1)}, u32[]{:S(2)}) %copy-start) | copy-done | bytes 2097176
  1.6 0.0 copy-start.1
  1.6 1.6 %copy-done.1 = bf16[1024,1024]{1,0:T(8,128)(2,1)S(1)} copy-done((bf16[1024,1024]{1,0:T(8,128)(2,1)S(1)}, bf16[1024,1024]{1,0:T(8,128)(2,1)}, u32[]{:S(2)}) %copy-start.1) | copy-done | bytes 2097176
  3.2 0.0 copy-start.2
  3.2 1.0 copy-done.2
  4.2 0.0 copy-start.3
  4.2 0.9 copy-done.3
  5.1 0.0 copy-start.4
  5.1 0.7 copy-done.4
  5.8 103.9 %shard_map.55 = bf16[6,32,1024]{2,1,0:T(8,128)(2,1)S(1)} custom-call(bf16[4,32,1024]{2,1,0:T(8,128)(2,1)S(1)} %bitcast.1, bf16[1,1024,1024]{2,1,0:T(8,128)(2,1)S(1)} %copy-done, bf16[1024,1024]{1,0:T(8,128)(2,1)S(1)} %copy-done.1, bf16[6,32,1024]{2,1,0:T(8,128)(2,1)S(1)} %copy-done.2, s32[1,8]{1,0:T(1,128)S(1)} %copy-done.4), custom_call_target="tpu_custom_call" | custom-call | tf_op jit(solution)/shard_map/pallas_call | solution.py:219
  109.7 0.7 copy.7
Async XLA Ops:
  0.0 1.6 %copy-start = (bf16[1,1024,1024]{2,1,0:T(8,128)(2,1)S(1)}, bf16[1,1024,1024]{2,1,0:T(8,128)(2,1)}, u32[]{:S(2)}) copy-start(bf16[1,1024,1024]{2,1,0:T(8,128)(2,1)} %coupling.1) | copy-start | bytes 6291460
  1.6 1.6 %copy-start.1 = (bf16[1024,1024]{1,0:T(8,128)(2,1)S(1)}, bf16[1024,1024]{1,0:T(8,128)(2,1)}, u32[]{:S(2)}) copy-start(bf16[1024,1024]{1,0:T(8,128)(2,1)} %inverse.1) | copy-start | bytes 6291460
  3.2 1.0 copy-start.2
  4.2 0.9 copy-start.3
  5.1 0.7 copy-start.4

commit v2 on v1

--- a/solution.py
+++ b/solution.py
@@ -13,17 +13,17 @@
 
 def kernel(
     patches, lags, steps, holders, width,
-    history, coupling, inverse, cotangent, targets, out,
+    history, coupling_far, inverse_far, cotangent_far, targets, out, coupling, inverse, cotangent,
     held_start, staged_start, chosen, product, terms, states, held, current, staged, listed, listed_scalar,
     list_send, list_recv, list_local, start_send, start_recv, place_start_send, chosen_recv,
-    term_send, term_recv, state_send, held_recv, place_send,
+    term_send, term_recv, state_send, held_recv, place_send, fetched, kept,
 ):
     patch = lax.axis_index("patch")
     lag = lax.axis_index("lag")
     rows = history.shape[1]
     unknowns = history.shape[2]
     depth = min(steps, lags)
-    tile = min(unknowns, 256)
+    tile = max(width, min(unknowns, 256))
 
     def columns(index):
         return pl.ds(pl.multiple_of(index * width, LANES), width)
@@ -37,6 +37,18 @@
             device_id=(to_patch, to_lag), device_id_type=MESH,
         ).start()
 
+    fetches = [
+        pltpu.make_async_copy(coupling_far.at[0], coupling, fetched.at[0]),
+        pltpu.make_async_copy(inverse_far, inverse, fetched.at[1]),
+        pltpu.make_async_copy(cotangent_far, cotangent, fetched.at[2]),
+    ]
+    for fetch in fetches:
+        fetch.start()
+
+    @pl.when(patch < holders)
+    def _():
+        pltpu.make_async_copy(history.at[:, :, columns(patch)], held_start.at[patch], kept).start()
+
     barrier = pltpu.get_barrier_semaphore()
     own = patch * lags + lag
 
@@ -60,10 +72,6 @@
 
     listed[lag] = targets[...]
 
-    @pl.when(patch < holders)
-    def _():
-        held_start[patch] = history[:, :, columns(patch)]
-
     await_bytes(listed.at[pl.ds(0, lags - 1)], list_recv)
     move = pltpu.make_async_copy(listed, listed_scalar, list_local)
     move.start()
@@ -71,6 +79,7 @@
 
     @pl.when(patch < holders)
     def _():
+        await_bytes(held_start.at[patch], kept)
         await_bytes(held_start.at[pl.ds(0, patches - 1)], start_recv)
 
         @pl.loop(0, depth)
@@ -84,7 +93,7 @@
                     to_patch = lax.rem(patch + offset, patches)
                     staged_start[step, to_patch] = held_start[listed_scalar[to_lag, 0, to_patch]]
                     src = staged_start.at[step, to_patch]
-                    dst = chosen.at[step, :, :, columns(patch)]
+                    dst = chosen.at[step, patch]
                     here = jnp.logical_and(step == 0, offset == 0)
 
                     @pl.when(here)
@@ -94,13 +103,18 @@
                     @pl.when(jnp.logical_not(here))
                     def _():
                         send(src, dst, place_start_send.at[step], chosen_recv.at[step], to_patch, to_lag)
+
+    for fetch in fetches:
+        fetch.wait()
 
     @pl.loop(0, steps)
     def _(step):
         await_bytes(chosen.at[step], chosen_recv.at[step])
-        picked = chosen[step].reshape(lags * rows, unknowns)
+        picked = jnp.concatenate(
+            [chosen[step, holder].reshape(lags * rows, width) for holder in range(holders)], axis=1
+        )
         for first in range(0, unknowns, tile):
-            part = jnp.dot(picked, coupling[0, :, first:first + tile], preferred_element_type=jnp.float32)
+            part = jnp.dot(picked, coupling[:, first:first + tile], preferred_element_type=jnp.float32)
             product[step, :, :, first:first + tile] = part.astype(jnp.bfloat16).reshape(lags, rows, tile)
 
         @pl.loop(1, lags)
@@ -115,8 +129,10 @@
         residual = total.astype(jnp.bfloat16)
         for first in range(0, unknowns, tile):
             state = jnp.dot(residual, inverse[:, first:first + tile], preferred_element_type=jnp.float32)
-            states[step, :, first:first + tile] = state.astype(jnp.bfloat16)
-        out[step] = states[step]
+            state = state.astype(jnp.bfloat16)
+            out[step, :, first:first + tile] = state
+            for part in range(0, tile, width):
+                states[step, (first + part) // width] = state[:, part:part + width]
 
         @pl.when(step + 1 < steps)
         def _():
@@ -125,13 +141,13 @@
                 @pl.when(holder != patch)
                 def _():
                     send(
-                        states.at[step, :, columns(holder)], held.at[step, patch],
+                        states.at[step, holder], held.at[step, patch],
                         state_send.at[step], held_recv.at[step], holder, lag,
                     )
 
             @pl.when(patch < holders)
             def _():
-                held[step, patch] = states[step, :, columns(patch)]
+                held[step, patch] = states[step, patch]
                 await_bytes(held.at[step, pl.ds(0, patches - 1)], held_recv.at[step])
                 current[...] = held[step]
 
@@ -146,7 +162,7 @@
                             to_patch = lax.rem(patch + offset, patches)
                             staged[step, to_lag, to_patch] = current[listed_scalar[to_lag, 0, to_patch]]
                             src = staged.at[step, to_lag, to_patch]
-                            dst = chosen.at[later, lag, :, columns(patch)]
+                            dst = chosen.at[later, patch, lag]
                             here = jnp.logical_and(to_lag == lag, offset == 0)
 
                             @pl.when(here)
@@ -214,27 +230,31 @@
     width = unknowns // holders
     depth = min(steps, lags)
     vmem = pl.BlockSpec(memory_space=pltpu.VMEM)
+    far = pl.BlockSpec(memory_space=pl.ANY)
     kind = history.dtype
     dma = pltpu.SemaphoreType.DMA
     return pl.pallas_call(
         functools.partial(kernel, patches, lags, steps, holders, width),
         out_shape=jax.ShapeDtypeStruct((steps, rows, unknowns), kind),
-        in_specs=[vmem] * 5,
+        in_specs=[far] * 4 + [vmem],
         out_specs=vmem,
         scratch_shapes=[
+            pltpu.VMEM(coupling.shape[1:], kind),
+            pltpu.VMEM(inverse.shape, kind),
+            pltpu.VMEM(cotangent.shape, kind),
             pltpu.VMEM((patches, lags, rows, width), kind),
             pltpu.VMEM((depth, patches, lags, rows, width), kind),
+            pltpu.VMEM((steps, holders, lags, rows, width), kind),
             pltpu.VMEM((steps, lags, rows, unknowns), kind),
             pltpu.VMEM((steps, lags, rows, unknowns), kind),
-            pltpu.VMEM((steps, lags, rows, unknowns), kind),
-            pltpu.VMEM((steps, rows, unknowns), kind),
+            pltpu.VMEM((steps, holders, rows, width), kind),
             pltpu.VMEM((steps, patches, rows, width), kind),
             pltpu.VMEM((patches, rows, width), kind),
             pltpu.VMEM((steps, lags, patches, rows, width), kind),
             pltpu.VMEM((lags, 1, patches), jnp.int32),
             pltpu.SMEM((lags, 1, patches), jnp.int32),
             dma, dma, dma, dma, dma, dma((depth,)), dma((steps,)),
-            dma((steps,)), dma((steps,)), dma((steps,)), dma((steps,)), dma((steps, lags)),
+            dma((steps,)), dma((steps,)), dma((steps,)), dma((steps,)), dma((steps, lags)), dma((3,)), dma,
         ],
         compiler_params=pltpu.CompilerParams(
             collective_id=0, has_side_effects=True, vmem_limit_bytes=48 * 1024 * 1024

time: 111 us -> 112 us (level)
  no operation moved by 1% of the time
where the time goes in v2:
time: 112 us; the launch traced here: 111 us
  Pallas kernels  105 us (94%)
  local copies, waits for them, and re-layouts  6.53 us (6%)
    pallas_call x1, Pallas kernels, on_device(): pl.pallas_call(functools.partial(kernel, patches, lags, steps, holders, w...  105 us
    unnamed x11, local copies, waits for them, and re-layouts  6.53 us

profile of v2, /device:TPU:0, one launch (start us, length us, event | category | flops | bytes accessed | tf_op | source)
XLA Modules:
  0.0 111.3 jit_solution(17217880425270275937)
XLA Ops:
  0.0 0.0 copy-start
  0.0 1.6 %copy-done = bf16[1,1024,1024]{2,1,0:T(8,128)(2,1)S(1)} copy-done((bf16[1,1024,1024]{2,1,0:T(8,128)(2,1)S(1)}, bf16[1,1024,1024]{2,1,0:T(8,128)(2,1)}, u32[]{:S(2)}) %copy-start) | copy-done | bytes 2097176
  1.6 0.0 copy-start.1
  1.6 1.6 %copy-done.1 = bf16[1024,1024]{1,0:T(8,128)(2,1)S(1)} copy-done((bf16[1024,1024]{1,0:T(8,128)(2,1)S(1)}, bf16[1024,1024]{1,0:T(8,128)(2,1)}, u32[]{:S(2)}) %copy-start.1) | copy-done | bytes 2097176
  3.2 0.0 copy-start.2
  3.2 1.0 copy-done.2
  4.2 0.0 copy-start.3
  4.2 0.9 copy-done.3
  5.1 0.0 copy-start.4
  5.1 0.7 copy-done.4
  5.8 104.8 %shard_map.55 = bf16[6,32,1024]{2,1,0:T(8,128)(2,1)S(1)} custom-call(bf16[4,32,1024]{2,1,0:T(8,128)(2,1)S(1)} %bitcast.1, bf16[1,1024,1024]{2,1,0:T(8,128)(2,1)S(1)} %copy-done, bf16[1024,1024]{1,0:T(8,128)(2,1)S(1)} %copy-done.1, bf16[6,32,1024]{2,1,0:T(8,128)(2,1)S(1)} %copy-done.2, s32[1,8]{1,0:T(1,128)S(1)} %copy-done.4), custom_call_target="tpu_custom_call" | custom-call | tf_op jit(solution)/shard_map/pallas_call | solution.py:236
  110.6 0.7 copy.7
Async XLA Ops:
  0.0 1.6 %copy-start = (bf16[1,1024,1024]{2,1,0:T(8,128)(2,1)S(1)}, bf16[1,1024,1024]{2,1,0:T(8,128)(2,1)}, u32[]{:S(2)}) copy-start(bf16[1,1024,1024]{2,1,0:T(8,128)(2,1)} %coupling_far.1) | copy-start | bytes 6291460
  1.6 1.6 %copy-start.1 = (bf16[1024,1024]{1,0:T(8,128)(2,1)S(1)}, bf16[1024,1024]{1,0:T(8,128)(2,1)}, u32[]{:S(2)}) copy-start(bf16[1024,1024]{1,0:T(8,128)(2,1)} %inverse_far.1) | copy-start | bytes 6291460
  3.2 1.0 copy-start.2
  4.2 0.9 copy-start.3
  5.1 0.7 copy-start.4

commit v3 on v2

v3 whole, which is shorter than its diff:
```python
import functools

import jax
import jax.numpy as jnp
from jax import lax
from jax.experimental import pallas as pl
from jax.experimental.pallas import tpu as pltpu
from jax.sharding import PartitionSpec as P

MESH = pl.DeviceIdType.MESH
LANES = 128


def kernel(
    patches, lags, steps, holders, width, span,
    history, coupling_far, inverse_far, cotangent_far, targets, out, coupling, inverse, cotangent,
    held_start, staged_start, chosen, product, residual, terms, states, held, current, staged, listed, listed_scalar,
    list_send, list_recv, list_local, start_send, start_recv, place_start_send, chosen_recv,
    term_send, term_recv, state_send, held_recv, place_send, fetched, kept, out_send, out_recv,
):
    patch = lax.axis_index("patch")
    lag = lax.axis_index("lag")
    groups, group_rows = chosen.shape[2:4]
    unknowns = history.shape[2]
    rows = out.shape[1]
    holds = jnp.logical_and(lax.rem(lag, span) == span - 1, patch < holders)
    depth = min(steps, lags)
    tile = max(width, min(unknowns, 256))

    def columns(index):
        return pl.ds(pl.multiple_of(index * width, LANES), width)

    def await_bytes(ref, semaphore):
        pltpu.make_async_copy(ref, ref, semaphore).wait()

    def send(src, dst, send_sem, recv_sem, to_patch, to_lag):
        pltpu.make_async_remote_copy(
            src_ref=src, dst_ref=dst, send_sem=send_sem, recv_sem=recv_sem,
            device_id=(to_patch, to_lag), device_id_type=MESH,
        ).start()

    fetches = [
        pltpu.make_async_copy(coupling_far.at[0], coupling, fetched.at[0]),
        pltpu.make_async_copy(inverse_far, inverse, fetched.at[1]),
        pltpu.make_async_copy(cotangent_far, cotangent, fetched.at[2]),
    ]
    for fetch in fetches:
        fetch.start()

    @pl.when(patch < holders)
    def _():
        pltpu.make_async_copy(history.at[:, :, columns(patch)], held_start.at[patch], kept).start()

    barrier = pltpu.get_barrier_semaphore()
    own = patch * lags + lag

    @pl.loop(1, patches * lags)
    def _(offset):
        other = lax.rem(own + offset, patches * lags)
        pl.semaphore_signal(barrier, inc=1, device_id=(other // lags, lax.rem(other, lags)), device_id_type=MESH)

    pl.semaphore_wait(barrier, patches * lags - 1)

    @pl.loop(1, lags)
    def _(offset):
        to_lag = lax.rem(lag + offset, lags)
        send(targets, listed.at[lag], list_send, list_recv, patch, to_lag)

    @pl.loop(0, holders)
    def _(holder):
        @pl.when(holder != patch)
        def _():
            send(history.at[:, :, columns(holder)], held_start.at[patch], start_send, start_recv, holder, lag)

    listed[lag] = targets[...]

    await_bytes(listed.at[pl.ds(0, lags - 1)], list_recv)
    move = pltpu.make_async_copy(listed, listed_scalar, list_local)
    move.start()
    move.wait()

    @pl.when(patch < holders)
    def _():
        await_bytes(held_start.at[patch], kept)
        await_bytes(held_start.at[pl.ds(0, patches - 1)], start_recv)

        @pl.loop(0, depth)
        def _(step):
            to_lag = lag + step

            @pl.when(to_lag < lags)
            def _():
                @pl.loop(0, patches)
                def _(offset):
                    to_patch = lax.rem(patch + offset, patches)
                    staged_start[step, to_patch] = held_start[listed_scalar[to_lag, 0, to_patch]]
                    src = staged_start.at[step, to_patch]
                    dst = chosen.at[step, patch]
                    here = jnp.logical_and(step == 0, offset == 0)

                    @pl.when(here)
                    def _():
                        pltpu.make_async_copy(src, dst, chosen_recv.at[step]).start()

                    @pl.when(jnp.logical_not(here))
                    def _():
                        send(src, dst, place_start_send.at[step], chosen_recv.at[step], to_patch, to_lag)

    for fetch in fetches:
        fetch.wait()

    @pl.loop(0, steps)
    def _(step):
        await_bytes(chosen.at[step], chosen_recv.at[step])
        picked = jnp.concatenate(
            [chosen[step, holder].reshape(groups * group_rows, width) for holder in range(holders)], axis=1
        )

        def driven(first):
            part = jnp.dot(picked, coupling[:, first:first + tile], preferred_element_type=jnp.float32)
            drive = cotangent[step, :, first:first + tile].astype(jnp.float32)
            blocks = part.reshape(lags, rows, tile)
            return [jnp.where(lag == block, drive, 0.0) - blocks[block] for block in range(lags)]

        @pl.when(lag > 0)
        def _():
            for first in range(0, unknowns, tile):
                for block, value in enumerate(driven(first)):
                    product[step, block, :, first:first + tile] = value.astype(jnp.bfloat16)
            send(product.at[step], terms.at[step, lag - 1], term_send.at[step], term_recv.at[step], patch, 0)

        @pl.when(lag == 0)
        def _():
            await_bytes(terms.at[step], term_recv.at[step])
            for first in range(0, unknowns, tile):
                for block, value in enumerate(driven(first)):
                    for other in range(lags - 1):
                        value = value + terms[step, other, block, :, first:first + tile].astype(jnp.float32)
                    residual[block, :, first:first + tile] = value.astype(jnp.bfloat16)
            drive = residual[...].reshape(lags * rows, unknowns)
            for first in range(0, unknowns, tile):
                state = jnp.dot(drive, inverse[:, first:first + tile], preferred_element_type=jnp.float32)
                state = state.astype(jnp.bfloat16)
                product[step, :, :, first:first + tile] = state.reshape(lags, rows, tile)
                for part in range(0, tile, width):
                    holder = (first + part) // width
                    states[step, holder] = state[:, part:part + width].reshape(groups, group_rows, width)

                    @pl.when(step + 1 < steps)
                    def _():
                        for group in range(groups):
                            send(
                                states.at[step, holder, group], held.at[step, patch],
                                state_send.at[step], held_recv.at[step], holder, group * span + span - 1,
                            )
            out[step] = product[step, 0]

            @pl.loop(1, lags)
            def _(block):
                send(product.at[step, block], out.at[step], out_send, out_recv, patch, block)

        @pl.when(jnp.logical_and(step > 0, holds))
        def _():
            done = step - 1
            await_bytes(held.at[done], held_recv.at[done])
            current[...] = held[done]

            @pl.loop(0, min(lags, steps - 1))
            def _(to_lag):
                later = step + to_lag

                @pl.when(later < steps)
                def _():
                    @pl.loop(0, patches)
                    def _(offset):
                        to_patch = lax.rem(patch + offset, patches)
                        staged[done, to_lag, to_patch] = current[listed_scalar[to_lag, 0, to_patch]]
                        src = staged.at[done, to_lag, to_patch]
                        dst = chosen.at[later, patch, lag // span]
                        here = jnp.logical_and(to_lag == lag, offset == 0)

                        @pl.when(here)
                        def _():
                            pltpu.make_async_copy(src, dst, chosen_recv.at[later]).start()

                        @pl.when(jnp.logical_not(here))
                        def _():
                            send(src, dst, place_send.at[done, to_lag], chosen_recv.at[later], to_patch, to_lag)

    await_bytes(listed.at[pl.ds(0, lags - 1)], list_send)

    @pl.when(patch < holders)
    def _():
        await_bytes(held_start.at[pl.ds(0, holders - 1)], start_send)

        @pl.loop(0, depth)
        def _(step):
            @pl.when(lag + step < lags)
            def _():
                @pl.when(step == 0)
                def _():
                    await_bytes(staged_start.at[step, pl.ds(0, patches - 1)], place_start_send.at[step])

                @pl.when(step > 0)
                def _():
                    await_bytes(staged_start.at[step], place_start_send.at[step])

    if holders < patches:
        @pl.when(patch >= holders)
        def _():
            await_bytes(held_start.at[pl.ds(0, holders)], start_send)

    @pl.when(lag == 0)
    def _():
        await_bytes(product.at[:, pl.ds(0, lags - 1)], out_send)

    @pl.when(lag > 0)
    def _():
        await_bytes(out, out_recv)

    @pl.loop(0, steps)
    def _(step):
        @pl.when(lag > 0)
        def _():
            await_bytes(product.at[step], term_send.at[step])

        @pl.when(jnp.logical_and(step + 1 < steps, lag == 0))
        def _():
            await_bytes(states.at[step], state_send.at[step])

        @pl.when(jnp.logical_and(step + 1 < steps, holds))
        def _():
            @pl.loop(0, min(lags, steps - 1))
            def _(to_lag):
                @pl.when(step + 1 + to_lag < steps)
                def _():
                    @pl.when(to_lag == lag)
                    def _():
                        await_bytes(staged.at[step, to_lag, pl.ds(0, patches - 1)], place_send.at[step, to_lag])

                    @pl.when(to_lag != lag)
                    def _():
                        await_bytes(staged.at[step, to_lag], place_send.at[step, to_lag])


def on_device(patches, lags, history, coupling, inverse, cotangent, targets):
    steps, rows, unknowns = cotangent.shape
    holders = min(patches, max(1, unknowns // LANES))
    width = unknowns // holders
    depth = min(steps, lags)
    span = 2
    groups, group_rows = lags // span, rows * span
    vmem = pl.BlockSpec(memory_space=pltpu.VMEM)
    far = pl.BlockSpec(memory_space=pl.ANY)
    kind = history.dtype
    dma = pltpu.SemaphoreType.DMA
    return pl.pallas_call(
        functools.partial(kernel, patches, lags, steps, holders, width, span),
        out_shape=jax.ShapeDtypeStruct((steps, rows, unknowns), kind),
        in_specs=[far] * 4 + [vmem],
        out_specs=vmem,
        scratch_shapes=[
            pltpu.VMEM(coupling.shape[1:], kind),
            pltpu.VMEM(inverse.shape, kind),
            pltpu.VMEM(cotangent.shape, kind),
            pltpu.VMEM((patches, groups, group_rows, width), kind),
            pltpu.VMEM((depth, patches, groups, group_rows, width), kind),
            pltpu.VMEM((steps, holders, groups, group_rows, width), kind),
            pltpu.VMEM((steps, lags, rows, unknowns), kind),
            pltpu.VMEM((lags, rows, unknowns), kind),
            pltpu.VMEM((steps, lags - 1, lags, rows, unknowns), kind),
            pltpu.VMEM((steps, holders, groups, group_rows, width), kind),
            pltpu.VMEM((steps, patches, group_rows, width), kind),
            pltpu.VMEM((patches, group_rows, width), kind),
            pltpu.VMEM((steps - 1, min(lags, steps - 1), patches, group_rows, width), kind),
            pltpu.VMEM((lags, 1, patches), jnp.int32),
            pltpu.SMEM((lags, 1, patches), jnp.int32),
            dma, dma, dma, dma, dma, dma((depth,)), dma((steps,)),
            dma((steps,)), dma((steps,)), dma((steps,)), dma((steps,)), dma((steps, lags)),
            dma((3,)), dma, dma, dma,
        ],
        compiler_params=pltpu.CompilerParams(
            collective_id=0, has_side_effects=True, vmem_limit_bytes=48 * 1024 * 1024
        ),
    )(history.reshape(groups, group_rows, unknowns), coupling, inverse, cotangent, targets)


def solution(mesh):
    placed = (
        P("lag", None, "patch"),
        P("lag", "patch", None),
        P("patch", None),
        P(None, "lag", "patch"),
        P("lag", None),
    )
    return jax.shard_map(
        functools.partial(on_device, mesh.shape["patch"], mesh.shape["lag"]),
        mesh=mesh, in_specs=placed, out_specs=P(None, "lag", "patch"), check_vma=False,
    )
```

time: 112 us -> 102 us (0.911)
  Pallas kernels: 105 us -> 95.5 us
    pallas_call x1, Pallas kernels: 105 us -> 95.5 us  [on_device(): pl.pallas_call(functools.partial(kernel, patches, lags, steps, holders, w...]
where the time goes in v3:
time: 102 us
  Pallas kernels  95.5 us (94%)
  local copies, waits for them, and re-layouts  6.53 us (6%)
    pallas_call x1, Pallas kernels, on_device(): pl.pallas_call(functools.partial(kernel, patches, lags, steps, holders, w...  95.5 us
    unnamed x11, local copies, waits for them, and re-layouts  6.53 us

profile of v3, /device:TPU:0, one launch (start us, length us, event | category | flops | bytes accessed | tf_op | source)
XLA Modules:
  0.0 102.1 jit_solution(7852448653878496291)
XLA Ops:
  0.0 0.0 copy-start
  0.0 1.6 %copy-done = bf16[1,1024,1024]{2,1,0:T(8,128)(2,1)S(1)} copy-done((bf16[1,1024,1024]{2,1,0:T(8,128)(2,1)S(1)}, bf16[1,1024,1024]{2,1,0:T(8,128)(2,1)}, u32[]{:S(2)}) %copy-start) | copy-done | bytes 2097176
  1.6 0.0 copy-start.1
  1.6 1.6 %copy-done.1 = bf16[1024,1024]{1,0:T(8,128)(2,1)S(1)} copy-done((bf16[1024,1024]{1,0:T(8,128)(2,1)S(1)}, bf16[1024,1024]{1,0:T(8,128)(2,1)}, u32[]{:S(2)}) %copy-start.1) | copy-done | bytes 2097176
  3.2 0.0 copy-start.2
  3.2 1.0 copy-done.2
  4.2 0.0 copy-start.3
  4.2 0.9 copy-done.3
  5.1 0.0 copy-start.4
  5.1 0.7 copy-done.4
  5.8 95.5 %shard_map.55 = bf16[6,32,1024]{2,1,0:T(8,128)(2,1)S(1)} custom-call(bf16[2,64,1024]{2,1,0:T(8,128)(2,1)S(1)} %bitcast.1, bf16[1,1024,1024]{2,1,0:T(8,128)(2,1)S(1)} %copy-done, bf16[1024,1024]{1,0:T(8,128)(2,1)S(1)} %copy-done.1, bf16[6,32,1024]{2,1,0:T(8,128)(2,1)S(1)} %copy-done.2, s32[1,8]{1,0:T(1,128)S(1)} %copy-done.4), custom_call_target="tpu_custom_call" | custom-call | tf_op jit(solution)/shard_map/pallas_call | solution.py:257
  101.3 0.7 copy.7
Async XLA Ops:
  0.0 1.6 %copy-start = (bf16[1,1024,1024]{2,1,0:T(8,128)(2,1)S(1)}, bf16[1,1024,1024]{2,1,0:T(8,128)(2,1)}, u32[]{:S(2)}) copy-start(bf16[1,1024,1024]{2,1,0:T(8,128)(2,1)} %coupling_far.1) | copy-start | bytes 6291460
  1.6 1.6 %copy-start.1 = (bf16[1024,1024]{1,0:T(8,128)(2,1)S(1)}, bf16[1024,1024]{1,0:T(8,128)(2,1)}, u32[]{:S(2)}) copy-start(bf16[1024,1024]{1,0:T(8,128)(2,1)} %inverse_far.1) | copy-start | bytes 6291460
  3.2 1.0 copy-start.2
  4.2 0.9 copy-start.3
  5.1 0.7 copy-start.4

commit v4 on v3

--- a/solution.py
+++ b/solution.py
@@ -127,14 +127,24 @@
             for first in range(0, unknowns, tile):
                 for block, value in enumerate(driven(first)):
                     product[step, block, :, first:first + tile] = value.astype(jnp.bfloat16)
-            send(product.at[step], terms.at[step, lag - 1], term_send.at[step], term_recv.at[step], patch, 0)
+
+            @pl.when(lax.rem(lag, span) == 1)
+            def _():
+                send(product.at[step], terms.at[step, 0], term_send.at[step], term_recv.at[step], patch, lag - 1)
+
+            @pl.when(lax.rem(lag, span) == 0)
+            def _():
+                await_bytes(terms.at[step, 0], term_recv.at[step])
+                both = product[step].astype(jnp.float32) + terms[step, 0].astype(jnp.float32)
+                product[step] = both.astype(jnp.bfloat16)
+                send(product.at[step], terms.at[step, lag // span], term_send.at[step], term_recv.at[step], patch, 0)
 
         @pl.when(lag == 0)
         def _():
             await_bytes(terms.at[step], term_recv.at[step])
             for first in range(0, unknowns, tile):
                 for block, value in enumerate(driven(first)):
-                    for other in range(lags - 1):
+                    for other in range(groups):
                         value = value + terms[step, other, block, :, first:first + tile].astype(jnp.float32)
                     residual[block, :, first:first + tile] = value.astype(jnp.bfloat16)
             drive = residual[...].reshape(lags * rows, unknowns)
@@ -146,13 +156,16 @@
                     holder = (first + part) // width
                     states[step, holder] = state[:, part:part + width].reshape(groups, group_rows, width)
 
-                    @pl.when(step + 1 < steps)
-                    def _():
-                        for group in range(groups):
-                            send(
-                                states.at[step, holder, group], held.at[step, patch],
-                                state_send.at[step], held_recv.at[step], holder, group * span + span - 1,
-                            )
+            @pl.when(step + 1 < steps)
+            def _():
+                for offset in range(holders):
+                    holder = lax.rem(patch + offset, holders)
+                    for group in range(groups):
+                        send(
+                            states.at[step, holder, group], held.at[step, patch],
+                            state_send.at[step], held_recv.at[step], holder, group * span + span - 1,
+                        )
+
             out[step] = product[step, 0]
 
             @pl.loop(1, lags)
@@ -171,10 +184,13 @@
 
                 @pl.when(later < steps)
                 def _():
-                    @pl.loop(0, patches)
+                    @pl.loop(0, patches, unroll=True)
+                    def _(to_patch):
+                        staged[done, to_lag, to_patch] = current[listed_scalar[to_lag, 0, to_patch]]
+
+                    @pl.loop(0, patches, unroll=True)
                     def _(offset):
                         to_patch = lax.rem(patch + offset, patches)
-                        staged[done, to_lag, to_patch] = current[listed_scalar[to_lag, 0, to_patch]]
                         src = staged.at[done, to_lag, to_patch]
                         dst = chosen.at[later, patch, lag // span]
                         here = jnp.logical_and(to_lag == lag, offset == 0)
@@ -268,7 +284,7 @@
             pltpu.VMEM((steps, holders, groups, group_rows, width), kind),
             pltpu.VMEM((steps, lags, rows, unknowns), kind),
             pltpu.VMEM((lags, rows, unknowns), kind),
-            pltpu.VMEM((steps, lags - 1, lags, rows, unknowns), kind),
+            pltpu.VMEM((steps, groups, lags, rows, unknowns), kind),
             pltpu.VMEM((steps, holders, groups, group_rows, width), kind),
             pltpu.VMEM((steps, patches, group_rows, width), kind),
             pltpu.VMEM((patches, group_rows, width), kind),

time: 102 us -> 100 us (0.980)
  Pallas kernels: 95.5 us -> 93.3 us
    pallas_call x1, Pallas kernels: 95.5 us -> 93.3 us  [on_device(): pl.pallas_call(functools.partial(kernel, patches, lags, steps, holders, w...]
where the time goes in v4:
time: 100 us; the launch traced here: 99.8 us
  Pallas kernels  93.3 us (93%)
  local copies, waits for them, and re-layouts  6.53 us (7%)
    pallas_call x1, Pallas kernels, on_device(): pl.pallas_call(functools.partial(kernel, patches, lags, steps, holders, w...  93.3 us
    unnamed x11, local copies, waits for them, and re-layouts  6.53 us

profile of v4, /device:TPU:0, one launch (start us, length us, event | category | flops | bytes accessed | tf_op | source)
XLA Modules:
  0.0 99.8 jit_solution(9019818897446823583)
XLA Ops:
  0.0 0.0 copy-start
  0.0 1.6 %copy-done = bf16[1,1024,1024]{2,1,0:T(8,128)(2,1)S(1)} copy-done((bf16[1,1024,1024]{2,1,0:T(8,128)(2,1)S(1)}, bf16[1,1024,1024]{2,1,0:T(8,128)(2,1)}, u32[]{:S(2)}) %copy-start) | copy-done | bytes 2097176
  1.6 0.0 copy-start.1
  1.6 1.6 %copy-done.1 = bf16[1024,1024]{1,0:T(8,128)(2,1)S(1)} copy-done((bf16[1024,1024]{1,0:T(8,128)(2,1)S(1)}, bf16[1024,1024]{1,0:T(8,128)(2,1)}, u32[]{:S(2)}) %copy-start.1) | copy-done | bytes 2097176
  3.2 0.0 copy-start.2
  3.2 1.0 copy-done.2
  4.2 0.0 copy-start.3
  4.2 0.9 copy-done.3
  5.1 0.0 copy-start.4
  5.1 0.7 copy-done.4
  5.8 93.3 %shard_map.55 = bf16[6,32,1024]{2,1,0:T(8,128)(2,1)S(1)} custom-call(bf16[2,64,1024]{2,1,0:T(8,128)(2,1)S(1)} %bitcast.1, bf16[1,1024,1024]{2,1,0:T(8,128)(2,1)S(1)} %copy-done, bf16[1024,1024]{1,0:T(8,128)(2,1)S(1)} %copy-done.1, bf16[6,32,1024]{2,1,0:T(8,128)(2,1)S(1)} %copy-done.2, s32[1,8]{1,0:T(1,128)S(1)} %copy-done.4), custom_call_target="tpu_custom_call" | custom-call | tf_op jit(solution)/shard_map/pallas_call | solution.py:273
  99.1 0.7 copy.7
Async XLA Ops:
  0.0 1.6 %copy-start = (bf16[1,1024,1024]{2,1,0:T(8,128)(2,1)S(1)}, bf16[1,1024,1024]{2,1,0:T(8,128)(2,1)}, u32[]{:S(2)}) copy-start(bf16[1,1024,1024]{2,1,0:T(8,128)(2,1)} %coupling_far.1) | copy-start | bytes 6291460
  1.6 1.6 %copy-start.1 = (bf16[1024,1024]{1,0:T(8,128)(2,1)S(1)}, bf16[1024,1024]{1,0:T(8,128)(2,1)}, u32[]{:S(2)}) copy-start(bf16[1024,1024]{1,0:T(8,128)(2,1)} %inverse_far.1) | copy-start | bytes 6291460
  3.2 1.0 copy-start.2
  4.2 0.9 copy-start.3
  5.1 0.7 copy-start.4
